TPU v7x, 256 devices: a whole 4x4x8 slice. The times are simulated.
256 devices in a mesh: dp: 16 (over x, y), seq: 16 (over z, core).
Axes of the slice: x: 4, y: 4, z: 8, core: 2. Of those that a mesh axis runs over, the one named last changes fastest.
Arguments:
- queries: bfloat16 [256, 128, 4096], P(('dp', 'seq')), parts along dimension 0, may hold values from -6 to 6
- outputs: bfloat16 [256, 128, 4096], P(('dp', 'seq')), parts along dimension 0, may hold values from -3 to 3
- out_grads: bfloat16 [256, 128, 4096], P(('dp', 'seq')), parts along dimension 0, may hold values from -12 to 12
- resp_keys: bfloat16 [256, 128, 512], P(('dp', 'seq')), parts along dimension 0, may hold values from -6 to 6
- resp_values: bfloat16 [256, 128, 512], P(('dp', 'seq')), parts along dimension 0, may hold values from -6 to 6
- lengths: int32 [256], P('dp'), parts along dimension 0, may hold values from 1 to 128, 1024 in all
- prompt_keys: bfloat16 [12288, 512], P(('dp', 'seq')), parts along dimension 0, may hold values from -6 to 6
- prompt_values: bfloat16 [12288, 512], P(('dp', 'seq')), parts along dimension 0, may hold values from -6 to 6
Outputs:
- query_grads: bfloat16 [256, 128, 4096], P(('dp', 'seq')), parts along dimension 0
- resp_key_grads: bfloat16 [256, 128, 512], P(('dp', 'seq')), parts along dimension 0
- resp_value_grads: bfloat16 [256, 128, 512], P(('dp', 'seq')), parts along dimension 0
- prompt_key_grads: bfloat16 [12288, 512], P(('dp', 'seq')), parts along dimension 0
- prompt_value_grads: bfloat16 [12288, 512], P(('dp', 'seq')), parts along dimension 0
There are 16 independent parts, one for each index of `dp`. A program takes and returns all parts, laid end to end along the dimension named above; each array names one. Nothing has to cross between parts.
All inputs are finite; a program needn't handle non-finite values.
Results may differ from a plain program's by a relative error of at most 0.0055.
Values may be sent and summed in bfloat16 or wider, within the bound.
A program may use at most 64 MiB of HBM per device.

v0:
```python
import jax
import jax.numpy as jnp
from jax import lax
from jax.sharding import PartitionSpec as P

HEAD_DIM = 128


def head_group(block, group_index, per_group, head_size):
    width = per_group * head_size
    sliced = lax.slice_in_dim(block, group_index * width, (group_index + 1) * width, axis=1)
    return sliced.reshape(block.shape[0], per_group, head_size)


def kv_column(block, group_index, head_size):
    return lax.slice_in_dim(block, group_index * head_size, (group_index + 1) * head_size, axis=1)


def scores_of(query_rows, key_block, softmax_scale):
    return (
        jnp.einsum("tgd,jd->gtj", query_rows, key_block, preferred_element_type=jnp.float32)
        * softmax_scale
    )


def block_grads(
    scores, grad_rows, row_delta, log_total, key_block, value_block, usable, softmax_scale
):
    probability = jnp.where(usable, jnp.exp(scores - log_total[:, :, None]), 0.0)
    prob_grad = jnp.einsum(
        "tgd,jd->gtj", grad_rows, value_block, preferred_element_type=jnp.float32
    )
    score_grad = (probability * (prob_grad - row_delta[:, :, None])).astype(jnp.bfloat16)
    weights = probability.astype(jnp.bfloat16)
    query_grad = (
        jnp.einsum("gtj,jd->tgd", score_grad, key_block, preferred_element_type=jnp.float32)
        * softmax_scale
    )
    return (query_grad, weights, score_grad)


def key_grads(weights, score_grad, query_rows, grad_rows, softmax_scale):
    value_grad = jnp.einsum("gtj,tgd->jd", weights, grad_rows, preferred_element_type=jnp.float32)
    key_grad = (
        jnp.einsum("gtj,tgd->jd", score_grad, query_rows, preferred_element_type=jnp.float32)
        * softmax_scale
    )
    return (key_grad, value_grad)


def own_path(
    query_all, output_all, grad_all, key_rows, value_rows, prompt_keys, prompt_values, length
):
    row_count = query_all.shape[0]
    kv_width = key_rows.shape[1]
    head_size = HEAD_DIM
    groups = kv_width // head_size
    per_group = query_all.shape[1] // kv_width
    softmax_scale = head_size ** (-0.5)
    position = lax.iota(jnp.int32, row_count)
    live_rows = position < length
    causal = position[None, :] <= position[:, None]
    prompt_usable = live_rows[None, :, None]
    resp_usable = (causal & live_rows[:, None])[None]
    query_list = [
        head_group(query_all, group_index, per_group, head_size) for group_index in range(groups)
    ]
    grad_list = [
        head_group(grad_all, group_index, per_group, head_size) for group_index in range(groups)
    ]
    delta_list = [
        jnp.sum(
            grad_list[group_index].astype(jnp.float32)
            * head_group(output_all, group_index, per_group, head_size).astype(jnp.float32),
            axis=2,
        ).T
        for group_index in range(groups)
    ]
    resp_key_list = [kv_column(key_rows, group_index, head_size) for group_index in range(groups)]
    resp_value_list = [
        kv_column(value_rows, group_index, head_size) for group_index in range(groups)
    ]
    resp_scores = [
        scores_of(query_list[group_index], resp_key_list[group_index], softmax_scale)
        for group_index in range(groups)
    ]
    all_keys, all_values = (
        lax.all_gather(prompt_keys, "seq", axis=0, tiled=True),
        lax.all_gather(prompt_values, "seq", axis=0, tiled=True),
    )
    dquery_list = []
    log_list = []
    weight_list = []
    sgrad_list = []
    for group_index in range(groups):
        key_block = kv_column(all_keys, group_index, head_size)
        value_block = kv_column(all_values, group_index, head_size)
        prompt_scores = scores_of(query_list[group_index], key_block, softmax_scale)
        masked_scores = jnp.where(causal[None], resp_scores[group_index], -1e30)
        top_score = jnp.maximum(jnp.max(prompt_scores, axis=2), jnp.max(masked_scores, axis=2))
        exp_total = jnp.sum(jnp.exp(prompt_scores - top_score[:, :, None]), axis=2)
        exp_total = exp_total + jnp.sum(
            jnp.where(causal[None], jnp.exp(resp_scores[group_index] - top_score[:, :, None]), 0.0),
            axis=2,
        )
        log_total = top_score + jnp.log(exp_total)
        query_grad, weights, score_grad = block_grads(
            prompt_scores,
            grad_list[group_index],
            delta_list[group_index],
            log_total,
            key_block,
            value_block,
            prompt_usable,
            softmax_scale,
        )
        dquery_list.append(query_grad)
        log_list.append(log_total)
        weight_list.append(weights)
        sgrad_list.append(score_grad)
    key_parts = []
    value_parts = []
    for prompt_group_index in range(groups):
        weight_cols = weight_list[prompt_group_index]
        sgrad_cols = sgrad_list[prompt_group_index]
        prompt_key_grad, prompt_value_grad = key_grads(
            weight_cols,
            sgrad_cols,
            query_list[prompt_group_index],
            grad_list[prompt_group_index],
            softmax_scale,
        )
        key_parts.append(prompt_key_grad)
        value_parts.append(prompt_value_grad)
    summed = lax.psum_scatter(
        jnp.concatenate(key_parts + value_parts, axis=1), "seq", scatter_dimension=0, tiled=True
    )
    query_parts = []
    resp_key_parts = []
    resp_value_parts = []
    for group_index in range(groups):
        query_grad, weights, score_grad = block_grads(
            resp_scores[group_index],
            grad_list[group_index],
            delta_list[group_index],
            log_list[group_index],
            resp_key_list[group_index],
            resp_value_list[group_index],
            resp_usable,
            softmax_scale,
        )
        key_grad, value_grad = key_grads(
            weights, score_grad, query_list[group_index], grad_list[group_index], softmax_scale
        )
        query_parts.append(
            (dquery_list[group_index] + query_grad).reshape(row_count, per_group * head_size)
        )
        resp_key_parts.append(key_grad)
        resp_value_parts.append(value_grad)
    query_grads = jnp.concatenate(query_parts, axis=1).astype(jnp.bfloat16)[None]
    resp_key_grads = jnp.concatenate(resp_key_parts, axis=1).astype(jnp.bfloat16)[None]
    resp_value_grads = jnp.concatenate(resp_value_parts, axis=1).astype(jnp.bfloat16)[None]
    prompt_key_grads = summed[:, :kv_width].astype(jnp.bfloat16)
    prompt_value_grads = summed[:, kv_width:].astype(jnp.bfloat16)
    return (query_grads, resp_key_grads, resp_value_grads, prompt_key_grads, prompt_value_grads)


def local(queries, outputs, out_grads, resp_keys, resp_values, lengths, prompt_keys, prompt_values):
    query_all = queries[0]
    output_all = outputs[0]
    grad_all = out_grads[0]
    key_rows = resp_keys[0]
    value_rows = resp_values[0]
    own_index = lax.axis_index("seq")
    length = jnp.sum(jnp.where(lax.iota(jnp.int32, lengths.shape[0]) == own_index, lengths, 0))
    results = own_path(
        query_all, output_all, grad_all, key_rows, value_rows, prompt_keys, prompt_values, length
    )
    return results


def solution(mesh):
    return jax.shard_map(
        local,
        mesh=mesh,
        in_specs=(
            P(("dp", "seq"), None, None),
            P(("dp", "seq"), None, None),
            P(("dp", "seq"), None, None),
            P(("dp", "seq"), None, None),
            P(("dp", "seq"), None, None),
            P("dp"),
            P(("dp", "seq"), None),
            P(("dp", "seq"), None),
        ),
        out_specs=(
            P(("dp", "seq"), None, None),
            P(("dp", "seq"), None, None),
            P(("dp", "seq"), None, None),
            P(("dp", "seq"), None),
            P(("dp", "seq"), None),
        ),
        check_vma=False,
    )
```

profile of v0, /device:TPU:2, one launch (start us, length us, event | category | flops | bytes accessed | tf_op | source)
XLA Modules:
  0.0 160.1 jit_solution(11860608578435821965)
XLA Ops:
  7.2 22.4 %all_gather.6 = bf16[768,512]{1,0:T(8,128)(2,1)S(1)} all-gather(bf16[48,512]{1,0:T(8,128)(2,1)} %param.14), channel_id=1, replica_groups=mesh['dp'=16,'seq'=16] {'seq'}, dimensions={0}, use_global_device_ids=true | all-gather | bytes 835584 | tf_op jit(solution)/shard_map/all_gather | solution.py:88
  29.6 1.9 %copy.128 = bf16[1,128,4096]{1,2,0:T(8,128)(2,1)S(1)} copy(bf16[1,128,4096]{2,1,0:T(8,128)(2,1)} %param.8) | data formatting | bytes 2097152 | tf_op args[0]
  32.1 2.8 %bitcast_reduce_fusion = (f32[8,128]{1,0:T(8,128)}, f32[768,128,8]{1,0,2:T(8,128)}) fusion(bf16[128,8,128]{0,2,1:T(8,128)(2,1)S(1)} %bitcast.445, bf16[768,512]{1,0:T(8,128)(2,1)S(1)} %all_gather.6), kind=kOutput, calls=%fused_computation.5 | convolution fusion | flops 202898432 | bytes 3608576 | tf_op jit(solution)/shard_map/tgd,jd->gtj/dot_general | solution.py:21
  34.9 2.8 %bitcast_reduce_fusion.1 = (f32[8,128]{1,0:T(8,128)}, f32[768,128,8]{1,0,2:T(8,128)}) fusion(bf16[128,8,128]{0,2,1:T(8,128)(2,1)S(1)} %bitcast.441, bf16[768,512]{1,0:T(8,128)(2,1)S(1)} %all_gather.6), kind=kOutput, calls=%fused_computation.15 | convolution fusion | flops 202898432 | bytes 3608576 | tf_op jit(solution)/shard_map/tgd,jd->gtj/dot_general | solution.py:21
  37.8 0.6 fusion.148
  38.4 1.2 iota_compare_fusion.1
  39.6 18.0 %all_gather.7 = bf16[768,512]{1,0:T(8,128)(2,1)} all-gather(bf16[48,512]{1,0:T(8,128)(2,1)S(1)} %copy-done.38), channel_id=1, replica_groups=mesh['dp'=16,'seq'=16] {'seq'}, dimensions={0}, use_global_device_ids=true | all-gather | bytes 835584 | tf_op jit(solution)/shard_map/all_gather | solution.py:89
  57.6 2.2 %bitcast_reduce_fusion.3 = (f32[8,128]{1,0:T(8,128)S(1)}, f32[768,128,8]{1,0,2:T(8,128)}) fusion(bf16[128,8,128]{0,2,1:T(8,128)(2,1)S(1)} %bitcast.432, bf16[768,512]{1,0:T(8,128)(2,1)S(1)} %all_gather.6), kind=kOutput, calls=%fused_computation.35 | convolution fusion | flops 202898432 | bytes 3608576 | tf_op jit(solution)/shard_map/tgd,jd->gtj/dot_general | solution.py:21
  60.1 1.8 %copy.133 = bf16[1,128,4096]{1,2,0:T(8,128)(2,1)S(1)} copy(bf16[1,128,4096]{2,1,0:T(8,128)(2,1)} %param.9) | data formatting | bytes 2097152 | tf_op args[1]
  61.9 1.0 fusion.163
  62.9 1.6 %copy.131 = bf16[1,128,4096]{1,2,0:T(8,128)(2,1)S(1)} copy(bf16[1,128,4096]{2,1,0:T(8,128)(2,1)} %param.10) | data formatting | bytes 2097152 | tf_op args[2]
  64.7 1.9 %bitcast_reduce_fusion.2 = (f32[8,128]{1,0:T(8,128)S(1)}, f32[768,128,8]{1,0,2:T(8,128)S(1)}) fusion(bf16[128,8,128]{0,2,1:T(8,128)(2,1)S(1)} %bitcast.436, bf16[768,512]{1,0:T(8,128)(2,1)} %copy-done.3), kind=kOutput, calls=%fused_computation.25 | convolution fusion | flops 202898432 | bytes 3608576 | tf_op jit(solution)/shard_map/tgd,jd->gtj/dot_general | solution.py:21
  68.6 0.8 copy-done.1
  71.7 1.0 fusion.19
  72.7 1.4 fusion.95
  74.1 1.0 fusion.13
  75.1 1.4 fusion.93
  76.5 1.0 fusion.7
  77.5 1.4 fusion.91
  78.9 0.9 fusion.1
  79.9 1.4 fusion.89
  81.3 1.5 fusion.59
  82.7 1.5 fusion.65
  84.2 1.5 fusion.71
  85.8 1.5 fusion.77
  87.2 3.5 %copy.243 = f32[768,1024]{1,0:T(8,128)} copy(f32[768,1024]{0,1:T(8,128)} %fusion.77) | data formatting | bytes 6291456
  90.8 0.8 broadcast_and_fusion
  91.7 0.9 fusion.112
  92.7 0.9 fusion.113
  93.6 1.0 fusion.114
  94.6 0.9 fusion.115
  95.6 0.8 copy.184
  96.3 1.2 fusion.81
  97.5 1.3 fusion.108
  98.8 1.2 fusion.83
  100.0 1.3 fusion.109
  101.3 1.2 fusion.85
  103.2 1.2 fusion.87
  104.7 0.8 copy.183
  105.5 1.9 %fusion.140 = f32[8,128,128]{1,2,0:T(8,128)S(1)} fusion(bf16[8,128,768]{1,2,0:T(8,128)(2,1)} %copy-done.14, bf16[768,512]{1,0:T(8,128)(2,1)S(1)} %copy-done.4), kind=kOutput, calls=%fused_computation.181 | convolution fusion | flops 201326592 | bytes 2293760 | tf_op jit(solution)/shard_map/gtj,jd->tgd/dot_general | solution.py:36
  108.6 0.9 copy.164
  109.4 1.9 %fusion.144 = f32[8,128,128]{1,2,0:T(8,128)S(1)} fusion(bf16[8,128,768]{1,2,0:T(8,128)(2,1)} %copy-done.17, bf16[768,512]{1,0:T(8,128)(2,1)S(1)} %copy-done.4), kind=kOutput, calls=%fused_computation.185 | convolution fusion | flops 201326592 | bytes 2293760 | tf_op jit(solution)/shard_map/gtj,jd->tgd/dot_general | solution.py:36
  111.6 0.9 copy.165
  113.3 2.1 %pad_maximum_fusion = bf16[1,128,4096]{2,1,0:T(8,128)(2,1)} fusion(bf16[1,128,1024]{2,1,0:T(8,128)(2,1)S(1)} %copy.166, bf16[1,128,1024]{2,1,0:T(8,128)(2,1)} %copy.165, bf16[1,128,1024]{2,1,0:T(8,128)(2,1)} %copy.164, bf16[1,128,1024]{2,1,0:T(8,128)(2,1)S(1)} %copy.163), kind=kLoop, calls=%fused_computation.136 | loop fusion | flops 4194304 | bytes 2097152 | tf_op jit(solution)/shard_map/concatenate | solution.py:160
  115.4 35.4 %reduce-scatter.4.cloned.1.call-done = f32[48,1024]{1,0:T(8,128)} async-done(((f32[768,1024]{1,0:T(8,128)}), f32[48,1024]{1,0:T(8,128)}) %reduce-scatter.4.cloned.1.call-update) | async-done | bytes 196624
  150.7 1.1 copy.244
  151.9 0.7 copy.186
  152.6 0.7 copy.185
  (136 shorter events, 8.4 us)
Async XLA Ops:
  7.2 24.5 %copy-start.37 = (bf16[1,128,512]{2,1,0:T(8,128)(2,1)S(1)}, bf16[1,128,512]{2,1,0:T(8,128)(2,1)}, u32[]{:S(2)}) copy-start(bf16[1,128,512]{2,1,0:T(8,128)(2,1)} %param.11) | copy-start | bytes 393220
  7.2 143.6 %reduce-scatter.4.cloned.1.call-start = ((), (), s32[]{:S(2)}) async-start(), calls=%async_computation.1 | async-start | bytes 3342336
  29.6 28.0 %copy-start.3 = (bf16[768,512]{1,0:T(8,128)(2,1)}, bf16[768,512]{1,0:T(8,128)(2,1)S(1)}, u32[]{:S(2)}) copy-start(bf16[768,512]{1,0:T(8,128)(2,1)S(1)} %all_gather.6) | copy-start | bytes 2359300
  31.6 6.1 %copy-start.8 = (bf16[128,1024]{0,1:T(8,128)(2,1)}, bf16[128,1024]{0,1:T(8,128)(2,1)S(1)}, u32[]{:S(2)}) copy-start(bf16[128,1024]{0,1:T(8,128)(2,1)S(1)} %get-tuple-element.35) | copy-start | bytes 786436
  31.6 6.1 %copy-start.10 = (bf16[128,1024]{0,1:T(8,128)(2,1)}, bf16[128,1024]{0,1:T(8,128)(2,1)S(1)}, u32[]{:S(2)}) copy-start(bf16[128,1024]{0,1:T(8,128)(2,1)S(1)} %get-tuple-element.36) | copy-start | bytes 786436
  31.6 33.0 %copy-start.5 = (bf16[128,1024]{0,1:T(8,128)(2,1)}, bf16[128,1024]{0,1:T(8,128)(2,1)S(1)}, u32[]{:S(2)}) copy-start(bf16[128,1024]{0,1:T(8,128)(2,1)S(1)} %get-tuple-element.37) | copy-start | bytes 786436
  32.1 5.7 %copy-start.50 = (s32[16]{0:T(128)S(1)}, s32[16]{0:T(128)}, u32[]{:S(2)}) copy-start(s32[16]{0:T(128)} %param.13) | copy-start | bytes 196
  32.1 7.5 %copy-start.38 = (bf16[48,512]{1,0:T(8,128)(2,1)S(1)}, bf16[48,512]{1,0:T(8,128)(2,1)}, u32[]{:S(2)}) copy-start(bf16[48,512]{1,0:T(8,128)(2,1)} %param.15) | copy-start | bytes 147460
  64.5 2.4 %copy-start.2 = (f32[768,128,8]{1,0,2:T(8,128)S(1)}, f32[768,128,8]{1,0,2:T(8,128)}, u32[]{:S(2)}) copy-start(f32[768,128,8]{1,0,2:T(8,128)} %get-tuple-element.48) | copy-start | bytes 9437188
  64.6 16.6 %copy-start.24 = (bf16[128,1024]{0,1:T(8,128)(2,1)}, bf16[128,1024]{0,1:T(8,128)(2,1)S(1)}, u32[]{:S(2)}) copy-start(bf16[128,1024]{0,1:T(8,128)(2,1)S(1)} %get-tuple-element.31) | copy-start | bytes 786436
  64.6 18.1 %copy-start.26 = (bf16[128,1024]{0,1:T(8,128)(2,1)}, bf16[128,1024]{0,1:T(8,128)(2,1)S(1)}, u32[]{:S(2)}) copy-start(bf16[128,1024]{0,1:T(8,128)(2,1)S(1)} %get-tuple-element.34) | copy-start | bytes 786436
  64.6 19.6 %copy-start.28 = (bf16[128,1024]{0,1:T(8,128)(2,1)}, bf16[128,1024]{0,1:T(8,128)(2,1)S(1)}, u32[]{:S(2)}) copy-start(bf16[128,1024]{0,1:T(8,128)(2,1)S(1)} %get-tuple-element.33) | copy-start | bytes 786436
  64.6 21.1 %copy-start.30 = (bf16[128,1024]{0,1:T(8,128)(2,1)}, bf16[128,1024]{0,1:T(8,128)(2,1)S(1)}, u32[]{:S(2)}) copy-start(bf16[128,1024]{0,1:T(8,128)(2,1)S(1)} %get-tuple-element.32) | copy-start | bytes 786436
  66.6 1.0 copy-start.6
  66.6 1.4 copy-start.47
  66.6 1.4 copy-start.48
  67.4 1.9 %copy-start.1 = (f32[768,128,8]{1,0,2:T(8,128)S(1)}, f32[768,128,8]{1,0,2:T(8,128)}, u32[]{:S(2)}) copy-start(f32[768,128,8]{1,0,2:T(8,128)} %get-tuple-element.55) | copy-start | bytes 9437188
  68.6 2.1 %copy-start = (f32[768,128,8]{1,0,2:T(8,128)S(1)}, f32[768,128,8]{1,0,2:T(8,128)}, u32[]{:S(2)}) copy-start(f32[768,128,8]{1,0,2:T(8,128)} %get-tuple-element.46) | copy-start | bytes 9437188
  69.9 1.3 copy-start.32
  69.9 1.3 copy-start.33
  69.9 1.3 copy-start.34
  69.9 1.3 copy-start.35
  69.9 1.8 %copy-start.36 = (bf16[768,512]{1,0:T(8,128)(2,1)S(1)}, bf16[768,512]{1,0:T(8,128)(2,1)}, u32[]{:S(2)}) copy-start(bf16[768,512]{1,0:T(8,128)(2,1)} %all_gather.7) | copy-start | bytes 2359300
  69.9 1.8 %copy-start.49 = (pred[128]{0:T(512)(128)(4,1)S(1)}, pred[128]{0:T(512)(128)(4,1)}, u32[]{:S(2)}) copy-start(pred[128]{0:T(512)(128)(4,1)} %iota_compare_fusion.1) | copy-start | bytes 388
  71.2 10.1 %copy-start.39 = (f32[8,128]{1,0:T(8,128)}, f32[8,128]{1,0:T(8,128)S(1)}, u32[]{:S(2)}) copy-start(f32[8,128]{1,0:T(8,128)S(1)} %log_add_fusion.3) | copy-start | bytes 12292
  71.6 2.4 %copy-start.43 = (f32[128,8]{0,1:T(8,128)}, f32[128,8]{0,1:T(8,128)S(1)}, u32[]{:S(2)}) copy-start(f32[128,8]{0,1:T(8,128)S(1)} %get-tuple-element.20) | copy-start | bytes 12292
  71.6 2.5 %copy-start.44 = (f32[128,8]{0,1:T(8,128)}, f32[128,8]{0,1:T(8,128)S(1)}, u32[]{:S(2)}) copy-start(f32[128,8]{0,1:T(8,128)S(1)} %get-tuple-element.21) | copy-start | bytes 12292
  71.7 4.8 %copy-start.45 = (f32[128,8]{0,1:T(8,128)}, f32[128,8]{0,1:T(8,128)S(1)}, u32[]{:S(2)}) copy-start(f32[128,8]{0,1:T(8,128)S(1)} %get-tuple-element.22) | copy-start | bytes 12292
  71.7 7.2 %copy-start.46 = (f32[128,8]{0,1:T(8,128)}, f32[128,8]{0,1:T(8,128)S(1)}, u32[]{:S(2)}) copy-start(f32[128,8]{0,1:T(8,128)S(1)} %get-tuple-element.23) | copy-start | bytes 12292
  72.7 1.4 copy-start.14
  74.1 8.7 %copy-start.40 = (f32[8,128]{1,0:T(8,128)}, f32[8,128]{1,0:T(8,128)S(1)}, u32[]{:S(2)}) copy-start(f32[8,128]{1,0:T(8,128)S(1)} %log_add_fusion.2) | copy-start | bytes 12292
  75.1 2.4 %copy-start.12 = (bf16[8,128,768]{1,2,0:T(8,128)(2,1)}, bf16[8,128,768]{1,2,0:T(8,128)(2,1)S(1)}, u32[]{:S(2)}) copy-start(bf16[8,128,768]{1,2,0:T(8,128)(2,1)S(1)} %fusion.13) | copy-start | bytes 4718596
  76.5 7.8 %copy-start.41 = (f32[8,128]{1,0:T(8,128)}, f32[8,128]{1,0:T(8,128)S(1)}, u32[]{:S(2)}) copy-start(f32[8,128]{1,0:T(8,128)S(1)} %get-tuple-element.57) | copy-start | bytes 12292
  76.5 9.3 %copy-start.42 = (f32[8,128]{1,0:T(8,128)}, f32[8,128]{1,0:T(8,128)S(1)}, u32[]{:S(2)}) copy-start(f32[8,128]{1,0:T(8,128)S(1)} %get-tuple-element.56) | copy-start | bytes 12292
  77.5 2.4 %copy-start.17 = (bf16[8,128,768]{1,2,0:T(8,128)(2,1)}, bf16[8,128,768]{1,2,0:T(8,128)(2,1)S(1)}, u32[]{:S(2)}) copy-start(bf16[8,128,768]{1,2,0:T(8,128)(2,1)S(1)} %fusion.7) | copy-start | bytes 4718596
  79.9 2.9 %copy-start.15 = (bf16[8,128,768]{1,2,0:T(8,128)(2,1)}, bf16[8,128,768]{1,2,0:T(8,128)(2,1)S(1)}, u32[]{:S(2)}) copy-start(bf16[8,128,768]{1,2,0:T(8,128)(2,1)S(1)} %fusion.1) | copy-start | bytes 4718596
  90.8 1.9 %copy-start.29 = (bf16[128,1024]{0,1:T(8,128)(2,1)S(1)}, bf16[128,1024]{0,1:T(8,128)(2,1)}, u32[]{:S(2)}) copy-start(bf16[128,1024]{0,1:T(8,128)(2,1)} %copy-done.28) | copy-start | bytes 786436
  90.8 2.8 %copy-start.27 = (bf16[128,1024]{0,1:T(8,128)(2,1)S(1)}, bf16[128,1024]{0,1:T(8,128)(2,1)}, u32[]{:S(2)}) copy-start(bf16[128,1024]{0,1:T(8,128)(2,1)} %copy-done.26) | copy-start | bytes 786436
  90.8 3.8 %copy-start.25 = (bf16[128,1024]{0,1:T(8,128)(2,1)S(1)}, bf16[128,1024]{0,1:T(8,128)(2,1)}, u32[]{:S(2)}) copy-start(bf16[128,1024]{0,1:T(8,128)(2,1)} %copy-done.24) | copy-start | bytes 786436
  93.6 8.9 %copy-start.7 = (bf16[128,1024]{0,1:T(8,128)(2,1)S(1)}, bf16[128,1024]{0,1:T(8,128)(2,1)}, u32[]{:S(2)}) copy-start(bf16[128,1024]{0,1:T(8,128)(2,1)} %copy-done.5) | copy-start | bytes 786436
  97.5 7.2 %copy-start.18 = (bf16[8,128,128]{1,2,0:T(8,128)(2,1)}, bf16[8,128,128]{1,2,0:T(8,128)(2,1)S(1)}, u32[]{:S(2)}) copy-start(bf16[8,128,128]{1,2,0:T(8,128)(2,1)S(1)} %fusion.81) | copy-start | bytes 786436
  97.5 8.0 %copy-start.4 = (bf16[768,512]{1,0:T(8,128)(2,1)S(1)}, bf16[768,512]{1,0:T(8,128)(2,1)}, u32[]{:S(2)}) copy-start(bf16[768,512]{1,0:T(8,128)(2,1)} %copy-done.3) | copy-start | bytes 2359300
  100.0 2.7 %copy-start.20 = (bf16[8,128,128]{1,2,0:T(8,128)(2,1)}, bf16[8,128,128]{1,2,0:T(8,128)(2,1)S(1)}, u32[]{:S(2)}) copy-start(bf16[8,128,128]{1,2,0:T(8,128)(2,1)S(1)} %fusion.83) | copy-start | bytes 786436
  104.4 3.4 %copy-start.13 = (bf16[8,128,768]{1,2,0:T(8,128)(2,1)S(1)}, bf16[8,128,768]{1,2,0:T(8,128)(2,1)}, u32[]{:S(2)}) copy-start(bf16[8,128,768]{1,2,0:T(8,128)(2,1)} %copy-done.12) | copy-start | bytes 4718596
  105.5 2.8 %copy-start.23 = (bf16[8,128,128]{1,2,0:T(8,128)(2,1)S(1)}, bf16[8,128,128]{1,2,0:T(8,128)(2,1)}, u32[]{:S(2)}) copy-start(bf16[8,128,128]{1,2,0:T(8,128)(2,1)} %copy-done.22) | copy-start | bytes 786436
  107.8 3.5 %copy-start.21 = (bf16[8,128,128]{1,2,0:T(8,128)(2,1)S(1)}, bf16[8,128,128]{1,2,0:T(8,128)(2,1)}, u32[]{:S(2)}) copy-start(bf16[8,128,128]{1,2,0:T(8,128)(2,1)} %copy-done.20) | copy-start | bytes 786436
  108.3 4.2 %copy-start.16 = (bf16[8,128,768]{1,2,0:T(8,128)(2,1)S(1)}, bf16[8,128,768]{1,2,0:T(8,128)(2,1)}, u32[]{:S(2)}) copy-start(bf16[8,128,768]{1,2,0:T(8,128)(2,1)} %copy-done.15) | copy-start | bytes 4718596
  109.4 3.5 %copy-start.19 = (bf16[8,128,128]{1,2,0:T(8,128)(2,1)S(1)}, bf16[8,128,128]{1,2,0:T(8,128)(2,1)}, u32[]{:S(2)}) copy-start(bf16[8,128,128]{1,2,0:T(8,128)(2,1)} %copy-done.18) | copy-start | bytes 786436
  (4 other events, 3.7 us)
Sparse Core Ops, SparseCore 0:
  90.9 59.7 reduce-scatter.3
where the time goes:
time: 161 us; the launch traced here: 160 us
  matrix products  43.3 us (27%)
  blocking collectives  40.4 us (25%)
  waiting for transfers between devices  35.4 us (22%)
  local copies, waits for them, and re-layouts  18.5 us (11%)
  between operations  15 us (9%)
  other arithmetic  7.58 us (5%)
    unnamed x2, waiting for transfers between devices  35.4 us
    all_gather x1, blocking collectives, own_path(): lax.all_gather(prompt_keys, 'seq', axis=0, tiled=True)  22.4 us
    all_gather x1, blocking collectives, own_path(): lax.all_gather(prompt_values, 'seq', axis=0, tiled=True)  18 us
    unnamed x111, local copies, waits for them, and re-layouts  15.3 us
    dot_general x8, matrix products, scores_of(): jnp.einsum('tgd,jd->gtj', query_rows, key_block, preferred_element_type=j...  10.8 us
    dot_general x8, matrix products, key_grads(): jnp.einsum('gtj,tgd->jd', weights, grad_rows, preferred_element_type=jnp....  9.7 us
    dot_general x8, matrix products, key_grads(): jnp.einsum('gtj,tgd->jd', score_grad, query_rows, preferred_element_type=...  8.57 us
    dot_general x8, matrix products, block_grads(): jnp.einsum('tgd,jd->gtj', grad_rows, value_block, preferred_element_type=...  8.56 us
  transfers between devices with their start and end apart: 1, of which 1 were waited for; matrix products, arithmetic and copies ran while one was open for 15% of the time, Pallas kernels for 0%

commit v1 on v0

v1 whole, which is shorter than its diff:
```python
import jax
import jax.numpy as jnp
from jax import lax
from jax.experimental import pallas as pl
from jax.experimental.pallas import tpu as pltpu
from jax.sharding import PartitionSpec as P

F32 = jnp.float32
BF16 = jnp.bfloat16
HEAD = 128
ROWS = 128
GROUPS = 4
PAIRS = 4
CHIPS = 8
OWN = 48
PROMPT = 2 * CHIPS * OWN
KEYS = PROMPT + ROWS
SCALE = HEAD**-0.5
SCALE2 = SCALE * 1.4426950408889634
BLOCK = 64


def dot(a, b):
    return jnp.dot(a, b, preferred_element_type=F32)


def dot_nt(a, b):
    return lax.dot_general(a, b, (((1,), (1,)), ((), ())), preferred_element_type=F32)


def kernel(
    q_hbm, o_hbm, g_hbm, rk_hbm, rv_hbm, len_ref, pk_hbm, pv_hbm,
    dq_hbm, drk_hbm, drv_hbm, dpk_hbm, dpv_hbm,
    q, o, g, rk, rv, kv, s_scr, dp_scr, p_scr, ds_scr, delta, acc, cp,
    sib_out, sib_in, st1_out, st1_in, st2_out, st2_in, dq, drk, drv, dpk, dpv,
    in_sem, own_sem, out_sem, gs_sem, gr_sem, ss_sem, sr_sem,
):
    me = lax.axis_index("seq")
    z = me // 2
    c = lax.rem(me, 2)
    sign = 1 - 2 * c
    sibling = me + sign

    def chip(k):
        return lax.rem(z + k + 16, CHIPS)

    def device(k):
        return chip(k) * 2 + c

    loads = []
    for i, (src, dst) in enumerate(((g_hbm, g), (o_hbm, o), (q_hbm, q), (rk_hbm, rk), (rv_hbm, rv))):
        loads.append(pltpu.make_async_copy(src.at[0], dst, in_sem.at[i]))
    own = kv.at[:, c, z]
    for h in range(GROUPS):
        cols = pl.ds(h * HEAD, HEAD)
        pltpu.make_async_copy(pk_hbm.at[:, cols], kv.at[h, c, z, :, pl.ds(0, HEAD)], own_sem).start()
        pltpu.make_async_copy(pv_hbm.at[:, cols], kv.at[h, c, z, :, pl.ds(HEAD, HEAD)], own_sem).start()
    for load in loads:
        load.start()

    barrier = pltpu.get_barrier_semaphore()
    for target in (device(1), device(-1), device(2), device(-2), sibling):
        pl.semaphore_signal(barrier, inc=1, device_id={"seq": target}, device_id_type=pl.DeviceIdType.MESH)
    pl.semaphore_wait(barrier, 5)
    pltpu.make_async_copy(own, own, own_sem).wait()

    def remote(src, dst, send, recv, target):
        return pltpu.make_async_remote_copy(
            src_ref=src, dst_ref=dst, send_sem=send, recv_sem=recv,
            device_id={"seq": target}, device_id_type=pl.DeviceIdType.MESH,
        )

    def gather(h, slot, origin, target):
        block = kv.at[h, c, chip(origin)]
        return remote(block, block, gs_sem.at[h, slot], gr_sem.at[h, slot], device(target))

    def gather_in(h, slot, origin):
        block = kv.at[h, c, chip(origin)]
        return remote(block, block, gs_sem.at[h, slot], gr_sem.at[h, slot], me)

    stage1 = ((0, 1), (1, -1), (2, 2), (3, -2))
    for h in range(GROUPS):
        for slot, step in stage1:
            gather(h, slot, 0, step).start()

    loads[0].wait()
    loads[1].wait()
    ones = jnp.ones((8, HEAD), BF16)

    def two(ref, pair):
        col = pl.multiple_of(pair * 2 * HEAD, 2 * HEAD)
        return jnp.concatenate([ref[:, pl.ds(col, HEAD)], ref[:, pl.ds(col + HEAD, HEAD)]], axis=0)

    def delta_pair(i, _):
        product = two(g, i).astype(F32) * two(o, i).astype(F32)
        high = product.astype(BF16)
        low = (product - high.astype(F32)).astype(BF16)
        delta[i] = dot_nt(ones, high) + dot_nt(ones, low)
        return 0

    lax.fori_loop(0, GROUPS * PAIRS, delta_pair, 0)
    for load in loads[2:]:
        load.wait()

    def forward(h, _):
        gather_in(h, 2, -2).wait_recv()
        gather(h, 4, -2, 1).start()
        gather_in(h, 3, 2).wait_recv()
        gather(h, 5, 2, -1).start()
        gather(h, 6, -2 * sign, 2 * sign).start()
        return 0

    lax.fori_loop(0, GROUPS, forward, 0)

    def half(h, core):
        return kv.at[h, core]

    def sib_gather(h, core):
        return remote(half(h, core), half(h, core), gs_sem.at[h, 7], gr_sem.at[h, 7], sibling)

    def pass_on(h):
        gather_in(h, 0, -1).wait_recv()
        gather_in(h, 1, 1).wait_recv()
        gather_in(h, 4, -3).wait_recv()
        gather_in(h, 5, 3).wait_recv()
        gather_in(h, 6, 4).wait_recv()
        sib_gather(h, c).start()

    def sib_scatter(h):
        return remote(sib_out.at[h], sib_in.at[h], ss_sem.at[h, 0], sr_sem.at[h, 0], sibling)

    def stage1_scatter(h, slot, target):
        return remote(st1_out.at[h, slot], st1_in.at[h, slot], ss_sem.at[h, 1 + slot], sr_sem.at[h, 1 + slot], target)

    def stage2_scatter(h, slot, target):
        return remote(st2_out.at[h, slot], st2_in.at[h, slot], ss_sem.at[h, 6 + slot], sr_sem.at[h, 6 + slot], target)

    first = ((0, 1, 3), (1, -1, -3), (2, 2 * sign, 4), (3, 1, 1), (4, -1, -1))

    def scatter_a(h):
        sib_out[h] = acc[1 - c].astype(BF16)
        sib_scatter(h).start()
        cp[h] = acc[c]

    def scatter_b(h):
        sib_scatter(h).wait_recv()
        cp[h] += sib_in[h].astype(F32)
        for slot, step, owner in first:
            st1_out[h, slot] = cp[h, chip(owner)].astype(BF16)
            stage1_scatter(h, slot, device(step)).start()

    def scatter_c(h):
        for slot in range(3):
            stage1_scatter(h, slot, me).wait_recv()
        cp[h, chip(2 * sign)] += st1_in[h, 2].astype(F32)
        st2_out[h, 0] = (cp[h, chip(2)] + st1_in[h, 0].astype(F32)).astype(BF16)
        stage2_scatter(h, 0, device(2)).start()
        st2_out[h, 1] = (cp[h, chip(-2)] + st1_in[h, 1].astype(F32)).astype(BF16)
        stage2_scatter(h, 1, device(-2)).start()

    def scatter_d(h):
        stage1_scatter(h, 3, me).wait_recv()
        stage1_scatter(h, 4, me).wait_recv()
        stage2_scatter(h, 0, me).wait_recv()
        stage2_scatter(h, 1, me).wait_recv()
        total = (
            cp[h, z] + st1_in[h, 3].astype(F32) + st1_in[h, 4].astype(F32)
            + st2_in[h, 0].astype(F32) + st2_in[h, 1].astype(F32)
        ).astype(BF16)
        col = pl.ds(pl.multiple_of(h * HEAD, HEAD), HEAD)
        dpk[:, col] = total[:, :HEAD]
        dpv[:, col] = total[:, HEAD:]

    token = lax.rem(lax.broadcasted_iota(jnp.int32, (1, 2 * ROWS), 1), ROWS)
    live = token < len_ref[me]
    causal = lax.broadcasted_iota(jnp.int32, (ROWS, 2 * ROWS), 0) <= lax.rem(
        lax.broadcasted_iota(jnp.int32, (ROWS, 2 * ROWS), 1), ROWS
    )

    def column(h):
        return pl.ds(pl.multiple_of(h * HEAD, HEAD), HEAD)

    def keys(h):
        return kv[h, :, :, :, pl.ds(0, HEAD)].reshape(PROMPT, HEAD)

    def values(h):
        return kv[h, :, :, :, pl.ds(HEAD, HEAD)].reshape(PROMPT, HEAD)

    def scores(h, p):
        b = p % 2
        q2 = two(q, h * PAIRS + p)
        g2 = two(g, h * PAIRS + p)
        s_scr[b, PROMPT:] = jnp.where(causal, dot_nt(rk[:, column(h)], q2), -1e30)
        s_scr[b, :PROMPT] = dot_nt(keys(h), q2)
        dp_scr[b, PROMPT:] = dot_nt(rv[:, column(h)], g2)
        dp_scr[b, :PROMPT] = dot_nt(values(h), g2)

    def softmax(h, p):
        b = p % 2
        top = jnp.full((8, 2 * ROWS), -1e30, F32)
        for r in range(0, KEYS, BLOCK):
            top = jnp.maximum(top, jnp.max(s_scr[b, r : r + BLOCK].reshape(BLOCK // 8, 8, 2 * ROWS), axis=0))
        top = jnp.max(top, axis=0, keepdims=True) * SCALE2
        total = jnp.zeros((8, 2 * ROWS), F32)
        for r in range(0, KEYS, BLOCK):
            e = jnp.exp2(s_scr[b, r : r + BLOCK] * SCALE2 - top)
            total = total + jnp.sum(e.reshape(BLOCK // 8, 8, 2 * ROWS), axis=0)
            s_scr[b, r : r + BLOCK] = e
        inverse = jnp.where(live, 1.0 / jnp.sum(total, axis=0, keepdims=True), 0.0)
        row_delta = delta[h * PAIRS + p][0:1]
        for r in range(0, KEYS, BLOCK):
            probability = s_scr[b, r : r + BLOCK] * inverse
            p_scr[p, r : r + BLOCK] = probability.astype(BF16)
            ds_scr[h * PAIRS + p, r : r + BLOCK] = (
                probability * (dp_scr[b, r : r + BLOCK] - row_delta)
            ).astype(BF16)

    pass_on(0)

    def group(h, _):
        sib_gather(h, 1 - c).wait_recv()
        scores(h, 0)
        for p in range(PAIRS):
            if p + 1 < PAIRS:
                scores(h, p + 1)
            softmax(h, p)
            if p == 1:
                @pl.when(h >= 1)
                def _():
                    scatter_b(h - 1)
            if p == 2:
                @pl.when(h < GROUPS - 1)
                def _():
                    pass_on(h + 1)
        g8 = jnp.concatenate([two(g, h * PAIRS + p) for p in range(PAIRS)], axis=0)
        q8 = jnp.concatenate([two(q, h * PAIRS + p) for p in range(PAIRS)], axis=0)
        dv = dot(jnp.concatenate([p_scr[p] for p in range(PAIRS)], axis=1), g8)
        dk = dot(jnp.concatenate([ds_scr[h * PAIRS + p] for p in range(PAIRS)], axis=1), q8) * SCALE
        acc[:, :, :, pl.ds(0, HEAD)] = dk[:PROMPT].reshape(2, CHIPS, OWN, HEAD)
        acc[:, :, :, pl.ds(HEAD, HEAD)] = dv[:PROMPT].reshape(2, CHIPS, OWN, HEAD)
        scatter_a(h)
        drk[:, column(h)] = dk[PROMPT:].astype(BF16)
        drv[:, column(h)] = dv[PROMPT:].astype(BF16)
        @pl.when(h >= 2)
        def _():
            scatter_c(h - 2)
        return 0

    lax.fori_loop(0, GROUPS, group, 0)

    out_rk = pltpu.make_async_copy(drk, drk_hbm.at[0], out_sem.at[0])
    out_rv = pltpu.make_async_copy(drv, drv_hbm.at[0], out_sem.at[1])
    out_rk.start()
    out_rv.start()

    def query_grads(h):
        kt = jnp.concatenate([keys(h), rk[:, column(h)]], axis=0).T
        for p in range(PAIRS):
            grad = dot(kt, ds_scr[h * PAIRS + p]) * SCALE
            col = pl.multiple_of((h * PAIRS + p) * 2 * HEAD, 2 * HEAD)
            dq[:, pl.ds(col, HEAD)] = grad[:, :ROWS].T.astype(BF16)
            dq[:, pl.ds(col + HEAD, HEAD)] = grad[:, ROWS:].T.astype(BF16)

    def dq_out(i):
        cols = pl.ds(i * 2048, 2048)
        return pltpu.make_async_copy(dq.at[:, cols], dq_hbm.at[0, :, cols], out_sem.at[2 + i])

    def query_loop(h, _):
        query_grads(h)
        return 0

    lax.fori_loop(0, 2, query_loop, 0)
    dq_out(0).start()
    scatter_b(3)
    scatter_c(2)
    lax.fori_loop(2, 4, query_loop, 0)
    dq_out(1).start()
    scatter_d(0)
    scatter_d(1)
    scatter_c(3)
    scatter_d(2)
    scatter_d(3)
    out_pk = pltpu.make_async_copy(dpk, dpk_hbm, out_sem.at[4])
    out_pv = pltpu.make_async_copy(dpv, dpv_hbm, out_sem.at[5])
    out_pk.start()
    out_pv.start()

    def drain(h, _):
        for slot, step in stage1:
            gather(h, slot, 0, step).wait_send()
        gather(h, 4, -2, 1).wait_send()
        gather(h, 5, 2, -1).wait_send()
        gather(h, 6, -2 * sign, 2 * sign).wait_send()
        sib_gather(h, c).wait_send()
        sib_scatter(h).wait_send()
        for slot, step, owner in first:
            stage1_scatter(h, slot, device(step)).wait_send()
        stage2_scatter(h, 0, device(2)).wait_send()
        stage2_scatter(h, 1, device(-2)).wait_send()
        return 0

    lax.fori_loop(0, GROUPS, drain, 0)
    for copy in (out_rk, out_rv, dq_out(0), dq_out(1), out_pk, out_pv):
        copy.wait()


def local(queries, outputs, out_grads, resp_keys, resp_values, lengths, prompt_keys, prompt_values):
    any_spec = pl.BlockSpec(memory_space=pl.ANY)
    wide = (ROWS, GROUPS * PAIRS * 2 * HEAD)
    narrow = (ROWS, GROUPS * HEAD)
    block = (OWN, 2 * HEAD)
    return pl.pallas_call(
        kernel,
        name="grads",
        out_shape=[
            jax.ShapeDtypeStruct((1,) + wide, BF16),
            jax.ShapeDtypeStruct((1,) + narrow, BF16),
            jax.ShapeDtypeStruct((1,) + narrow, BF16),
            jax.ShapeDtypeStruct((OWN, GROUPS * HEAD), BF16),
            jax.ShapeDtypeStruct((OWN, GROUPS * HEAD), BF16),
        ],
        in_specs=[any_spec] * 5 + [pl.BlockSpec(memory_space=pltpu.SMEM)] + [any_spec] * 2,
        out_specs=[any_spec] * 5,
        scratch_shapes=[
            pltpu.VMEM(wide, BF16),
            pltpu.VMEM(wide, BF16),
            pltpu.VMEM(wide, BF16),
            pltpu.VMEM(narrow, BF16),
            pltpu.VMEM(narrow, BF16),
            pltpu.VMEM((GROUPS, 2, CHIPS) + block, BF16),
            pltpu.VMEM((2, KEYS, 2 * ROWS), F32),
            pltpu.VMEM((2, KEYS, 2 * ROWS), F32),
            pltpu.VMEM((PAIRS, KEYS, 2 * ROWS), BF16),
            pltpu.VMEM((GROUPS * PAIRS, KEYS, 2 * ROWS), BF16),
            pltpu.VMEM((GROUPS * PAIRS, 8, 2 * ROWS), F32),
            pltpu.VMEM((2, CHIPS) + block, F32),
            pltpu.VMEM((GROUPS, CHIPS) + block, F32),
            pltpu.VMEM((GROUPS, CHIPS) + block, BF16),
            pltpu.VMEM((GROUPS, CHIPS) + block, BF16),
            pltpu.VMEM((GROUPS, 5) + block, BF16),
            pltpu.VMEM((GROUPS, 5) + block, BF16),
            pltpu.VMEM((GROUPS, 2) + block, BF16),
            pltpu.VMEM((GROUPS, 2) + block, BF16),
            pltpu.VMEM(wide, BF16),
            pltpu.VMEM(narrow, BF16),
            pltpu.VMEM(narrow, BF16),
            pltpu.VMEM((OWN, GROUPS * HEAD), BF16),
            pltpu.VMEM((OWN, GROUPS * HEAD), BF16),
            pltpu.SemaphoreType.DMA((5,)),
            pltpu.SemaphoreType.DMA,
            pltpu.SemaphoreType.DMA((6,)),
            pltpu.SemaphoreType.DMA((GROUPS, 8)),
            pltpu.SemaphoreType.DMA((GROUPS, 8)),
            pltpu.SemaphoreType.DMA((GROUPS, 8)),
            pltpu.SemaphoreType.DMA((GROUPS, 8)),
        ],
        compiler_params=pltpu.CompilerParams(
            collective_id=0, has_side_effects=True, vmem_limit_bytes=56 * 2**20
        ),
        cost_estimate=pl.CostEstimate(flops=4700000000, bytes_accessed=5000000, transcendentals=3670016),
    )(queries, outputs, out_grads, resp_keys, resp_values, lengths, prompt_keys, prompt_values)


def solution(mesh):
    rows = P(("dp", "seq"), None, None)
    prompt = P(("dp", "seq"), None)
    return jax.shard_map(
        local,
        mesh=mesh,
        in_specs=(rows, rows, rows, rows, rows, P("dp"), prompt, prompt),
        out_specs=(rows, rows, rows, prompt, prompt),
        check_vma=False,
    )
```

time: 161 us -> 50.4 us (0.31)
  Pallas kernels: 0 us -> 43.9 us
  matrix products: 43.3 us -> 0 us
  blocking collectives: 40.4 us -> 0 us
  waiting for transfers between devices: 35.4 us -> 0 us
  between operations: 15 us -> 0.66 us
  local copies, waits for them, and re-layouts: 18.5 us -> 5.51 us
  other arithmetic: 7.58 us -> 0 us
    pallas_call x0 -> x1, Pallas kernels: none -> 43.9 us  [local(): pl.pallas_call(kernel, name='grads', out_shape=[jax.ShapeDtypeStruct((1,)...]
    dot_general x40 -> x0, matrix products: 43.3 us -> none  [the longest x8 10.8 us: scores_of(): jnp.einsum('tgd,jd->gtj', query_rows, key_block, preferred_element_type=j...]
    all_gather x2 -> x0, blocking collectives: 40.4 us -> none  [the longest x1 22.4 us: own_path(): lax.all_gather(prompt_keys, 'seq', axis=0, tiled=True)]
    unnamed x2 -> x0, waiting for transfers between devices: 35.4 us -> none
    unnamed x111 -> x13, local copies, waits for them, and re-layouts: 15.3 us -> 5.51 us
    reduce_sum x7 -> x0, other arithmetic: 3.41 us -> none  [the longest x4 2.09 us: own_path(): exp_total = jnp.sum(jnp.exp(prompt_scores - top_score[:, :, None]), axis=2)]
    concatenate x3 -> x0, other arithmetic: 2.11 us -> none  [the longest x1 2.08 us: own_path(): jnp.concatenate(query_parts, axis=1).astype(jnp.bfloat16)[None]]
    concatenate x4 -> x0, local copies, waits for them, and re-layouts: 2.01 us -> none  [own_path(): jnp.concatenate(query_parts, axis=1).astype(jnp.bfloat16)[None]]
  transfers between devices with their start and end apart: 1 -> 0, of which waited for: 1 -> 0; matrix products, arithmetic and copies ran while one was open for 15% -> 0% of each run, Pallas kernels for 0% -> 0%
where the time goes in v1:
time: 50.4 us; the launch traced here: 50 us
  Pallas kernels  43.9 us (87%)
  local copies, waits for them, and re-layouts  5.51 us (11%)
  between operations  0.66 us (1%)
    pallas_call x1, Pallas kernels, local(): pl.pallas_call(kernel, name='grads', out_shape=[jax.ShapeDtypeStruct((1,)...  43.9 us
    unnamed x13, local copies, waits for them, and re-layouts  5.51 us

profile of v1, /device:TPU:2, one launch (start us, length us, event | category | flops | bytes accessed | tf_op | source)
XLA Modules:
  0.0 50.0 jit_solution(4898399406035674914)
XLA Ops:
  0.6 43.9 %grads.1 = (bf16[1,128,4096]{2,1,0:T(8,128)(2,1)}, bf16[1,128,512]{2,1,0:T(8,128)(2,1)}, bf16[1,128,512]{2,1,0:T(8,128)(2,1)}, bf16[48,512]{1,0:T(8,128)(2,1)}, bf16[48,512]{1,0:T(8,128)(2,1)}) custom-call(bf16[1,128,4096]{2,1,0:T(8,128)(2,1)} %q_hbm.1, bf16[1,128,4096]{2,1,0:T(8,128)(2,1)} %o_hbm.1, bf16[1,128,4096]{2,1,0:T(8,128)(2,1)} %g_hbm.1, ...), custom_call_target="tpu_custom_call" | custom-call | flops 4700000256 | bytes 5000000 | tf_op jit(solution)/shard_map/grads/pallas_call | solution.py:312
  44.5 0.0 copy-start.1
  44.5 2.3 %copy.18 = bf16[1,128,4096]{2,1,0:T(8,128)(2,1)} copy(bf16[1,128,4096]{2,1,0:T(8,128)(2,1)} %get-tuple-element.10) | data formatting | bytes 2097152
  46.9 0.0 copy-done.1
  46.9 0.0 copy-start
  46.9 0.7 %copy.19 = bf16[1,128,512]{2,1,0:T(8,128)(2,1)} copy(bf16[1,128,512]{2,1,0:T(8,128)(2,1)S(1)} %copy-done.1) | data formatting | bytes 262144
  47.5 0.3 copy-done
  47.8 0.0 copy-start.3
  47.8 0.7 %copy.20 = bf16[1,128,512]{2,1,0:T(8,128)(2,1)} copy(bf16[1,128,512]{2,1,0:T(8,128)(2,1)S(1)} %copy-done) | data formatting | bytes 262144
  48.5 0.1 copy-done.3
  48.6 0.0 copy-start.2
  48.6 0.6 %copy.21 = bf16[48,512]{1,0:T(8,128)(2,1)} copy(bf16[48,512]{1,0:T(8,128)(2,1)S(1)} %copy-done.3) | data formatting | bytes 98304
  49.2 0.2 copy-done.2
  49.4 0.6 %copy.22 = bf16[48,512]{1,0:T(8,128)(2,1)} copy(bf16[48,512]{1,0:T(8,128)(2,1)S(1)} %copy-done.2) | data formatting | bytes 98304
Async XLA Ops:
  44.5 2.3 %copy-start.1 = (bf16[1,128,512]{2,1,0:T(8,128)(2,1)S(1)}, bf16[1,128,512]{2,1,0:T(8,128)(2,1)}, u32[]{:S(2)}) copy-start(bf16[1,128,512]{2,1,0:T(8,128)(2,1)} %get-tuple-element.11) | copy-start | bytes 393220
  46.9 1.0 %copy-start = (bf16[1,128,512]{2,1,0:T(8,128)(2,1)S(1)}, bf16[1,128,512]{2,1,0:T(8,128)(2,1)}, u32[]{:S(2)}) copy-start(bf16[1,128,512]{2,1,0:T(8,128)(2,1)} %get-tuple-element.12) | copy-start | bytes 393220
  47.8 0.8 %copy-start.3 = (bf16[48,512]{1,0:T(8,128)(2,1)S(1)}, bf16[48,512]{1,0:T(8,128)(2,1)}, u32[]{:S(2)}) copy-start(bf16[48,512]{1,0:T(8,128)(2,1)} %get-tuple-element.13) | copy-start | bytes 147460
  48.6 0.8 %copy-start.2 = (bf16[48,512]{1,0:T(8,128)(2,1)S(1)}, bf16[48,512]{1,0:T(8,128)(2,1)}, u32[]{:S(2)}) copy-start(bf16[48,512]{1,0:T(8,128)(2,1)} %get-tuple-element.14) | copy-start | bytes 147460

commit v2 on v1

v2 whole, which is shorter than its diff:
```python
import functools

import jax
import jax.numpy as jnp
from jax import lax
from jax.experimental import pallas as pl
from jax.experimental.pallas import tpu as pltpu
from jax.sharding import PartitionSpec as P

F32 = jnp.float32
BF16 = jnp.bfloat16
HEAD = 128
ROWS = 128
GROUPS = 4
PAIRS = 4
WIDE = 2 * ROWS
CHIPS = 8
OWN = 48
HALF = CHIPS * OWN
PROMPT = 2 * HALF
KEYS = PROMPT + ROWS
BLOCK = 256
SCALE = HEAD**-0.5
SCALE2 = SCALE * 1.4426950408889634
MESH = pl.DeviceIdType.MESH


def dot(a, b):
    return jnp.dot(a, b, preferred_element_type=F32)


def dot_nt(a, b):
    return lax.dot_general(a, b, (((1,), (1,)), ((), ())), preferred_element_type=F32)


def fold(x, op):
    return op(x.reshape(x.shape[0] // 8, 8, x.shape[1]), axis=0)


def weave(*lists):
    steps = max(len(entry) for entry in lists)
    done = [0] * len(lists)
    for step in range(steps):
        for i, entry in enumerate(lists):
            while done[i] < len(entry) and done[i] * steps < (step + 1) * len(entry):
                entry[done[i]]()
                done[i] += 1


def kernel(
    q_hbm, o_hbm, g_hbm, rk_hbm, rv_hbm, len_ref, pk_hbm, pv_hbm,
    dq_hbm, drk_hbm, drv_hbm, dpk_hbm, dpv_hbm,
    q, o, g, rk, rv, kv, s_scr, rs_scr, rdp_scr, p_scr, rp_scr, ds_scr, delta, acc, cp,
    sib_out, sib_in, st1_out, st1_in, st2_out, st2_in, dq, drk, drv, dpk, dpv,
    in_sem, own_sem, out_sem, gs_sem, gr_sem, ss_sem, sr_sem,
):
    me = lax.axis_index("seq")
    z = me // 2
    c = lax.rem(me, 2)
    sign = 1 - 2 * c
    sibling = me + sign

    def chip(k):
        return lax.rem(z + k + 16, CHIPS)

    def device(k):
        return chip(k) * 2 + c

    def rows_of(zz):
        return pl.ds(pl.multiple_of(zz * OWN, 16), OWN)

    def half_of(core):
        return pl.ds(pl.multiple_of(core * HALF, HALF), HALF)

    def block_of(zz):
        return pl.ds(pl.multiple_of((c * CHIPS + zz) * OWN, 16), OWN)

    loads = []
    for i, (src, dst) in enumerate(((g_hbm, g), (o_hbm, o), (q_hbm, q), (rk_hbm, rk), (rv_hbm, rv))):
        loads.append(pltpu.make_async_copy(src.at[0], dst, in_sem.at[i]))
    own = kv.at[:, block_of(z)]
    for h in range(GROUPS):
        cols = pl.ds(h * HEAD, HEAD)
        pltpu.make_async_copy(pk_hbm.at[:, cols], kv.at[h, block_of(z), pl.ds(0, HEAD)], own_sem).start()
        pltpu.make_async_copy(pv_hbm.at[:, cols], kv.at[h, block_of(z), pl.ds(HEAD, HEAD)], own_sem).start()
    for load in loads:
        load.start()

    barrier = pltpu.get_barrier_semaphore()
    for target in (device(1), device(-1), device(2), device(-2), sibling):
        pl.semaphore_signal(barrier, inc=1, device_id={"seq": target}, device_id_type=MESH)
    pl.semaphore_wait(barrier, 5)
    pltpu.make_async_copy(own, own, own_sem).wait()

    def remote(src, dst, send, recv, target):
        return pltpu.make_async_remote_copy(
            src_ref=src, dst_ref=dst, send_sem=send, recv_sem=recv,
            device_id={"seq": target}, device_id_type=MESH,
        )

    def gather(h, slot, origin, target):
        block = kv.at[h, block_of(chip(origin))]
        return remote(block, block, gs_sem.at[h, slot], gr_sem.at[h, slot], device(target))

    def gather_wait(h, slot, origin):
        gather(h, slot, origin, 1).wait_recv()

    near = ((0, 1), (1, -1), (2, 2), (3, -2))

    def gather_near(h):
        for slot, step in near:
            gather(h, slot, 0, step).start()

    def gather_far(h):
        gather_wait(h, 2, -2)
        gather(h, 4, -2, 1).start()
        gather_wait(h, 3, 2)
        gather(h, 5, 2, -1).start()
        gather(h, 6, -2 * sign, 2 * sign).start()

    def sib_gather(h, core):
        part = kv.at[h, half_of(core)]
        return remote(part, part, gs_sem.at[h, 7], gr_sem.at[h, 7], sibling)

    def pass_on(h):
        for slot, origin in ((0, -1), (1, 1), (4, -3), (5, 3), (6, 4)):
            gather_wait(h, slot, origin)
        sib_gather(h, c).start()

    def sib_scatter(h):
        return remote(sib_out.at[h], sib_in.at[h], ss_sem.at[h, 0], sr_sem.at[h, 0], sibling)

    def scatter1(h, slot, step):
        return remote(
            st1_out.at[h, slot], st1_in.at[h, slot], ss_sem.at[h, 1 + slot], sr_sem.at[h, 1 + slot], device(step)
        )

    def scatter2(h, slot, step):
        return remote(
            st2_out.at[h, slot], st2_in.at[h, slot], ss_sem.at[h, 6 + slot], sr_sem.at[h, 6 + slot], device(step)
        )

    first = ((0, 1, 3), (1, -1, -3), (2, 2 * sign, 4), (3, 1, 1), (4, -1, -1))

    def scatter_a(h):
        sib_out[h] = acc[half_of(1 - c)].astype(BF16)
        sib_scatter(h).start()
        cp[h] = acc[half_of(c)]

    def scatter_b(h):
        sib_scatter(h).wait_recv()
        cp[h] += sib_in[h].astype(F32)
        for slot, step, owner in first:
            st1_out[h, slot] = cp[h, rows_of(chip(owner))].astype(BF16)
            scatter1(h, slot, step).start()

    def scatter_c(h):
        for slot in range(3):
            scatter1(h, slot, 1).wait_recv()
        cp[h, rows_of(chip(2 * sign))] += st1_in[h, 2].astype(F32)
        for slot, step in ((0, 2), (1, -2)):
            st2_out[h, slot] = (cp[h, rows_of(chip(step))] + st1_in[h, slot].astype(F32)).astype(BF16)
            scatter2(h, slot, step).start()

    def scatter_d(h):
        for slot in (3, 4):
            scatter1(h, slot, 1).wait_recv()
        for slot in (0, 1):
            scatter2(h, slot, 1).wait_recv()
        total = (
            cp[h, rows_of(z)] + st1_in[h, 3].astype(F32) + st1_in[h, 4].astype(F32)
            + st2_in[h, 0].astype(F32) + st2_in[h, 1].astype(F32)
        ).astype(BF16)
        dpk[:, column(h)] = total[:, :HEAD]
        dpv[:, column(h)] = total[:, HEAD:]

    token = lax.rem(lax.broadcasted_iota(jnp.int32, (1, WIDE), 1), ROWS)
    live = token < len_ref[me]
    causal = lax.broadcasted_iota(jnp.int32, (ROWS, WIDE), 0) <= lax.rem(
        lax.broadcasted_iota(jnp.int32, (ROWS, WIDE), 1), ROWS
    )
    ones = jnp.ones((8, HEAD), BF16)

    def column(h):
        return pl.ds(pl.multiple_of(h * HEAD, HEAD), HEAD)

    def two(ref, i):
        col = pl.multiple_of(i * WIDE, WIDE)
        return jnp.concatenate([ref[:, pl.ds(col, HEAD)], ref[:, pl.ds(col + HEAD, HEAD)]], axis=0)

    def prepare(i, _):
        q2, g2, o2 = two(q, i), two(g, i), two(o, i)
        product = g2.astype(F32) * o2.astype(F32)
        high = product.astype(BF16)
        low = (product - high.astype(F32)).astype(BF16)
        delta[i] = dot_nt(ones, high) + dot_nt(ones, low)
        col = column(i // PAIRS)
        rs_scr[i] = jnp.where(causal, dot_nt(rk[:, col], q2), -1e30)
        rdp_scr[i] = dot_nt(rv[:, col], g2)
        return 0

    gather_near(0)
    gather_near(1)
    for load in loads:
        load.wait()
    lax.fori_loop(0, GROUPS * PAIRS, prepare, 0)
    gather_far(0)
    gather_near(2)
    gather_far(1)
    gather_near(3)
    pass_on(0)

    def scores(h, p, state):
        i, b = h * PAIRS + p, p % 2
        q2 = two(q, i)

        def begin():
            state["top"] = fold(rs_scr[i], jnp.max)

        def step(r):
            rows = slice(r, r + BLOCK)
            s = dot_nt(kv[h, rows, :HEAD], q2)
            s_scr[b, rows] = s
            state["top"] = jnp.maximum(state["top"], fold(s, jnp.max))

        return [begin] + [functools.partial(step, r) for r in range(0, PROMPT, BLOCK)]

    def exponents(h, p, state):
        i, b = h * PAIRS + p, p % 2

        def begin():
            state["shift"] = jnp.max(state["top"], axis=0, keepdims=True) * SCALE2
            e = jnp.exp2(rs_scr[i] * SCALE2 - state["shift"])
            rs_scr[i] = e
            state["total"] = fold(e, jnp.sum)

        def step(r):
            rows = slice(r, r + BLOCK)
            e = jnp.exp2(s_scr[b, rows] * SCALE2 - state["shift"])
            s_scr[b, rows] = e
            state["total"] = state["total"] + fold(e, jnp.sum)

        return [begin] + [functools.partial(step, r) for r in range(0, PROMPT, BLOCK)]

    def score_grads(h, p, state):
        i, b = h * PAIRS + p, p % 2
        g2 = two(g, i)
        row_delta = delta[i][0:1]

        def begin():
            total = jnp.sum(state["total"], axis=0, keepdims=True)
            state["inverse"] = jnp.where(live, 1.0 / total, 0.0)
            probability = rs_scr[i] * state["inverse"]
            rp_scr[i] = probability.astype(BF16)
            ds_scr[i, PROMPT:] = (probability * (rdp_scr[i] - row_delta)).astype(BF16)

        def step(r):
            rows = slice(r, r + BLOCK)
            prob_grad = dot_nt(kv[h, rows, HEAD:], g2)
            probability = s_scr[b, rows] * state["inverse"]
            p_scr[p, rows] = probability.astype(BF16)
            ds_scr[i, rows] = (probability * (prob_grad - row_delta)).astype(BF16)

        return [begin] + [functools.partial(step, r) for r in range(0, PROMPT, BLOCK)]

    def prompt_grads(h, p):
        i = h * PAIRS + p

        def keys():
            a = dot(ds_scr[i, :PROMPT], two(q, i)) * SCALE
            acc[:, :HEAD] = a if p == 0 else acc[:, :HEAD] + a

        def values():
            a = dot(p_scr[p], two(g, i))
            acc[:, HEAD:] = a if p == 0 else acc[:, HEAD:] + a

        return [values, keys]

    def group(h, _):
        sib_gather(h, 1 - c).wait_recv()
        state, pending = {}, []
        for entry in scores(h, 0, state):
            entry()
        for p in range(PAIRS):
            following, ahead = {}, []
            if p + 1 < PAIRS:
                ahead = scores(h, p + 1, following)
            weave(exponents(h, p, state), ahead)
            weave(score_grads(h, p, state), pending)
            pending = prompt_grads(h, p)
            state = following
            if p < 2:
                @pl.when(h == 0)
                def _():
                    gather_far(2 + p)
            if p == 1:
                @pl.when(h >= 1)
                def _():
                    scatter_b(h - 1)

                @pl.when(h < GROUPS - 1)
                def _():
                    pass_on(h + 1)
            if p == 2:
                @pl.when(h >= 2)
                def _():
                    scatter_c(h - 2)
        for entry in pending:
            entry()
        scatter_a(h)
        return 0

    lax.fori_loop(0, GROUPS, group, 0)

    def finish_group(h, _):
        col = column(h)
        g8 = jnp.concatenate([two(g, h * PAIRS + p) for p in range(PAIRS)], axis=0)
        q8 = jnp.concatenate([two(q, h * PAIRS + p) for p in range(PAIRS)], axis=0)
        p8 = jnp.concatenate([rp_scr[h * PAIRS + p] for p in range(PAIRS)], axis=1)
        ds8 = jnp.concatenate([ds_scr[h * PAIRS + p, PROMPT:] for p in range(PAIRS)], axis=1)
        drv[:, col] = dot(p8, g8).astype(BF16)
        drk[:, col] = (dot(ds8, q8) * SCALE).astype(BF16)
        kt = jnp.concatenate([kv[h, :, :HEAD], rk[:, col]], axis=0).T
        for p in range(PAIRS):
            grad = dot(kt, ds_scr[h * PAIRS + p]) * SCALE
            at = pl.multiple_of((h * PAIRS + p) * WIDE, WIDE)
            dq[:, pl.ds(at, HEAD)] = grad[:, :ROWS].T.astype(BF16)
            dq[:, pl.ds(at + HEAD, HEAD)] = grad[:, ROWS:].T.astype(BF16)
        return 0

    def dq_out(i):
        cols = pl.ds(i * 2048, 2048)
        return pltpu.make_async_copy(dq.at[:, cols], dq_hbm.at[0, :, cols], out_sem.at[2 + i])

    out_rk = pltpu.make_async_copy(drk, drk_hbm.at[0], out_sem.at[0])
    out_rv = pltpu.make_async_copy(drv, drv_hbm.at[0], out_sem.at[1])
    out_pk = pltpu.make_async_copy(dpk, dpk_hbm, out_sem.at[4])
    out_pv = pltpu.make_async_copy(dpv, dpv_hbm, out_sem.at[5])
    lax.fori_loop(0, 2, finish_group, 0)
    dq_out(0).start()
    scatter_b(3)
    scatter_c(2)
    lax.fori_loop(2, 4, finish_group, 0)
    dq_out(1).start()
    out_rk.start()
    out_rv.start()
    scatter_d(0)
    scatter_d(1)

    def drain(h, _):
        for slot, step in near:
            gather(h, slot, 0, step).wait_send()
        gather(h, 4, -2, 1).wait_send()
        gather(h, 5, 2, -1).wait_send()
        gather(h, 6, -2 * sign, 2 * sign).wait_send()
        sib_gather(h, c).wait_send()
        sib_scatter(h).wait_send()
        return 0

    lax.fori_loop(0, GROUPS, drain, 0)
    scatter_c(3)
    scatter_d(2)
    scatter_d(3)
    out_pk.start()
    out_pv.start()

    def drain_scatter(h, _):
        for slot, step, owner in first:
            scatter1(h, slot, step).wait_send()
        scatter2(h, 0, 2).wait_send()
        scatter2(h, 1, -2).wait_send()
        return 0

    lax.fori_loop(0, GROUPS, drain_scatter, 0)
    for copy in (out_rk, out_rv, dq_out(0), dq_out(1), out_pk, out_pv):
        copy.wait()


def finish(*refs):
    sources, targets, held = refs[:5], refs[5:10], refs[10:15]
    in_sem, out_sem = refs[15:]
    parts = [(0, (slice(None), slice(None), pl.ds(part * 1024, 1024))) for part in range(4)]
    parts += [(i, ()) for i in range(1, 5)]

    def view(ref, index):
        return ref.at[index] if index else ref

    loads = [
        pltpu.make_async_copy(view(sources[i], at), view(held[i], at), in_sem.at[n])
        for n, (i, at) in enumerate(parts)
    ]
    stores = [
        pltpu.make_async_copy(view(held[i], at), view(targets[i], at), out_sem.at[n])
        for n, (i, at) in enumerate(parts)
    ]
    for load in loads:
        load.start()
    for load, store in zip(loads, stores):
        load.wait()
        store.start()
    for store in stores:
        store.wait()


def local(queries, outputs, out_grads, resp_keys, resp_values, lengths, prompt_keys, prompt_values):
    any_spec = pl.BlockSpec(memory_space=pl.ANY)
    pairs = GROUPS * PAIRS
    wide = (ROWS, pairs * WIDE)
    narrow = (ROWS, GROUPS * HEAD)
    block = (OWN, 2 * HEAD)
    half = (HALF, 2 * HEAD)
    shapes = [
        jax.ShapeDtypeStruct((1,) + wide, BF16),
        jax.ShapeDtypeStruct((1,) + narrow, BF16),
        jax.ShapeDtypeStruct((1,) + narrow, BF16),
        jax.ShapeDtypeStruct((OWN, GROUPS * HEAD), BF16),
        jax.ShapeDtypeStruct((OWN, GROUPS * HEAD), BF16),
    ]
    results = pl.pallas_call(
        kernel,
        name="grads",
        out_shape=shapes,
        in_specs=[any_spec] * 5 + [pl.BlockSpec(memory_space=pltpu.SMEM)] + [any_spec] * 2,
        out_specs=[any_spec] * 5,
        scratch_shapes=[
            pltpu.VMEM(wide, BF16),
            pltpu.VMEM(wide, BF16),
            pltpu.VMEM(wide, BF16),
            pltpu.VMEM(narrow, BF16),
            pltpu.VMEM(narrow, BF16),
            pltpu.VMEM((GROUPS, PROMPT, 2 * HEAD), BF16),
            pltpu.VMEM((2, PROMPT, WIDE), F32),
            pltpu.VMEM((pairs, ROWS, WIDE), F32),
            pltpu.VMEM((pairs, ROWS, WIDE), F32),
            pltpu.VMEM((PAIRS, PROMPT, WIDE), BF16),
            pltpu.VMEM((pairs, ROWS, WIDE), BF16),
            pltpu.VMEM((pairs, KEYS, WIDE), BF16),
            pltpu.VMEM((pairs, 8, WIDE), F32),
            pltpu.VMEM((PROMPT, 2 * HEAD), F32),
            pltpu.VMEM((GROUPS,) + half, F32),
            pltpu.VMEM((GROUPS,) + half, BF16),
            pltpu.VMEM((GROUPS,) + half, BF16),
            pltpu.VMEM((GROUPS, 5) + block, BF16),
            pltpu.VMEM((GROUPS, 5) + block, BF16),
            pltpu.VMEM((GROUPS, 2) + block, BF16),
            pltpu.VMEM((GROUPS, 2) + block, BF16),
            pltpu.VMEM(wide, BF16),
            pltpu.VMEM(narrow, BF16),
            pltpu.VMEM(narrow, BF16),
            pltpu.VMEM((OWN, GROUPS * HEAD), BF16),
            pltpu.VMEM((OWN, GROUPS * HEAD), BF16),
            pltpu.SemaphoreType.DMA((5,)),
            pltpu.SemaphoreType.DMA,
            pltpu.SemaphoreType.DMA((6,)),
            pltpu.SemaphoreType.DMA((GROUPS, 8)),
            pltpu.SemaphoreType.DMA((GROUPS, 8)),
            pltpu.SemaphoreType.DMA((GROUPS, 8)),
            pltpu.SemaphoreType.DMA((GROUPS, 8)),
        ],
        compiler_params=pltpu.CompilerParams(
            collective_id=0, has_side_effects=True, vmem_limit_bytes=56 * 2**20
        ),
        cost_estimate=pl.CostEstimate(flops=4700000000, bytes_accessed=5000000, transcendentals=3670016),
    )(queries, outputs, out_grads, resp_keys, resp_values, lengths, prompt_keys, prompt_values)
    return pl.pallas_call(
        finish,
        name="finish",
        out_shape=shapes,
        in_specs=[any_spec] * 5,
        out_specs=[any_spec] * 5,
        scratch_shapes=[pltpu.VMEM(shape.shape, shape.dtype) for shape in shapes]
        + [pltpu.SemaphoreType.DMA((8,))] * 2,
    )(*results)


def solution(mesh):
    rows = P(("dp", "seq"), None, None)
    prompt = P(("dp", "seq"), None)
    return jax.shard_map(
        local,
        mesh=mesh,
        in_specs=(rows, rows, rows, rows, rows, P("dp"), prompt, prompt),
        out_specs=(rows, rows, rows, prompt, prompt),
        check_vma=False,
    )
```

time: 50.4 us -> 44.4 us (0.88)
  local copies, waits for them, and re-layouts: 5.51 us -> 0 us
    unnamed x13 -> x0, local copies, waits for them, and re-layouts: 5.51 us -> none
    pallas_call x1 -> x2, Pallas kernels: 43.9 us -> 43.6 us  [the longest x1 41.5 us: local(): pl.pallas_call(kernel, name='grads', out_shape=shapes, in_specs=[any_spec...]
where the time goes in v2:
time: 44.4 us; the launch traced here: 44.3 us
  Pallas kernels  43.6 us (98%)
  between operations  0.64 us (1%)
    pallas_call x1, Pallas kernels, local(): pl.pallas_call(kernel, name='grads', out_shape=shapes, in_specs=[any_spec...  41.5 us
    pallas_call x1, Pallas kernels, local(): pl.pallas_call(finish, name='finish', out_shape=shapes, in_specs=[any_spe...  2.16 us

profile of v2, /device:TPU:2, one launch (start us, length us, event | category | flops | bytes accessed | tf_op | source)
XLA Modules:
  0.0 44.3 jit_solution(4649747268320806271)
XLA Ops:
  0.6 41.5 %grads.1 = (bf16[1,128,4096]{2,1,0:T(8,128)(2,1)}, bf16[1,128,512]{2,1,0:T(8,128)(2,1)}, bf16[1,128,512]{2,1,0:T(8,128)(2,1)}, bf16[48,512]{1,0:T(8,128)(2,1)}, bf16[48,512]{1,0:T(8,128)(2,1)}) custom-call(bf16[1,128,4096]{2,1,0:T(8,128)(2,1)} %q_hbm.1, bf16[1,128,4096]{2,1,0:T(8,128)(2,1)} %o_hbm.1, bf16[1,128,4096]{2,1,0:T(8,128)(2,1)} %g_hbm.1, ...), custom_call_target="tpu_custom_call" | custom-call | flops 4700000256 | bytes 5000000 | tf_op jit(solution)/shard_map/grads/pallas_call | solution.py:419
  42.1 2.2 %finish.1 = (bf16[1,128,4096]{2,1,0:T(8,128)(2,1)}, bf16[1,128,512]{2,1,0:T(8,128)(2,1)}, bf16[1,128,512]{2,1,0:T(8,128)(2,1)}, bf16[48,512]{1,0:T(8,128)(2,1)}, bf16[48,512]{1,0:T(8,128)(2,1)}) custom-call(bf16[1,128,4096]{2,1,0:T(8,128)(2,1)} %get-tuple-element.10.refs_0_, bf16[1,128,512]{2,1,0:T(8,128)(2,1)} %get-tuple-element.11.refs_1_, ...), custom_call_target="tpu_custom_call" | custom-call | tf_op jit(solution)/shard_map/finish/pallas_call | solution.py:465

commit v3 on v2

--- a/solution.py
+++ b/solution.py
@@ -48,11 +48,11 @@
 
 
 def kernel(
-    q_hbm, o_hbm, g_hbm, rk_hbm, rv_hbm, len_ref, pk_hbm, pv_hbm,
+    q_hbm, o_hbm, g_hbm, rk_hbm, rv_hbm, len_hbm, pk_hbm, pv_hbm,
     dq_hbm, drk_hbm, drv_hbm, dpk_hbm, dpv_hbm,
     q, o, g, rk, rv, kv, s_scr, rs_scr, rdp_scr, p_scr, rp_scr, ds_scr, delta, acc, cp,
     sib_out, sib_in, st1_out, st1_in, st2_out, st2_in, dq, drk, drv, dpk, dpv,
-    in_sem, own_sem, out_sem, gs_sem, gr_sem, ss_sem, sr_sem,
+    len_ref, in_sem, own_sem, out_sem, gs_sem, gr_sem, ss_sem, sr_sem,
 ):
     me = lax.axis_index("seq")
     z = me // 2
@@ -78,6 +78,7 @@
     loads = []
     for i, (src, dst) in enumerate(((g_hbm, g), (o_hbm, o), (q_hbm, q), (rk_hbm, rk), (rv_hbm, rv))):
         loads.append(pltpu.make_async_copy(src.at[0], dst, in_sem.at[i]))
+    loads.append(pltpu.make_async_copy(len_hbm, len_ref, in_sem.at[5]))
     own = kv.at[:, block_of(z)]
     for h in range(GROUPS):
         cols = pl.ds(h * HEAD, HEAD)
@@ -105,7 +106,7 @@
     def gather_wait(h, slot, origin):
         gather(h, slot, origin, 1).wait_recv()
 
-    near = ((0, 1), (1, -1), (2, 2), (3, -2))
+    near = ((2, 2), (3, -2), (0, 1), (1, -1))
 
     def gather_near(h):
         for slot, step in near:
@@ -175,7 +176,6 @@
         dpv[:, column(h)] = total[:, HEAD:]
 
     token = lax.rem(lax.broadcasted_iota(jnp.int32, (1, WIDE), 1), ROWS)
-    live = token < len_ref[me]
     causal = lax.broadcasted_iota(jnp.int32, (ROWS, WIDE), 0) <= lax.rem(
         lax.broadcasted_iota(jnp.int32, (ROWS, WIDE), 1), ROWS
     )
@@ -209,6 +209,8 @@
     gather_far(1)
     gather_near(3)
     pass_on(0)
+
+    live = token < len_ref[me]
 
     def scores(h, p, state):
         i, b = h * PAIRS + p, p % 2
@@ -339,8 +341,8 @@
     lax.fori_loop(0, 2, finish_group, 0)
     dq_out(0).start()
     scatter_b(3)
+    lax.fori_loop(2, 4, finish_group, 0)
     scatter_c(2)
-    lax.fori_loop(2, 4, finish_group, 0)
     dq_out(1).start()
     out_rk.start()
     out_rv.start()
@@ -420,7 +422,7 @@
         kernel,
         name="grads",
         out_shape=shapes,
-        in_specs=[any_spec] * 5 + [pl.BlockSpec(memory_space=pltpu.SMEM)] + [any_spec] * 2,
+        in_specs=[any_spec] * 8,
         out_specs=[any_spec] * 5,
         scratch_shapes=[
             pltpu.VMEM(wide, BF16),
@@ -449,7 +451,8 @@
             pltpu.VMEM(narrow, BF16),
             pltpu.VMEM((OWN, GROUPS * HEAD), BF16),
             pltpu.VMEM((OWN, GROUPS * HEAD), BF16),
-            pltpu.SemaphoreType.DMA((5,)),
+            pltpu.SMEM((2 * CHIPS,), jnp.int32),
+            pltpu.SemaphoreType.DMA((6,)),
             pltpu.SemaphoreType.DMA,
             pltpu.SemaphoreType.DMA((6,)),
             pltpu.SemaphoreType.DMA((GROUPS, 8)),

time: 44.4 us -> 44.1 us (level)
  Pallas kernels: 43.6 us -> 43 us
    pallas_call x1, Pallas kernels: 41.5 us -> 40.8 us  [local(): pl.pallas_call(kernel, name='grads', out_shape=shapes, in_specs=[any_spec...]
where the time goes in v3:
time: 44.1 us; the launch traced here: 43.6 us
  Pallas kernels  43 us (98%)
  between operations  0.64 us (1%)
    pallas_call x1, Pallas kernels, local(): pl.pallas_call(kernel, name='grads', out_shape=shapes, in_specs=[any_spec...  40.8 us
    pallas_call x1, Pallas kernels, local(): pl.pallas_call(finish, name='finish', out_shape=shapes, in_specs=[any_spe...  2.16 us

profile of v3, /device:TPU:2, one launch (start us, length us, event | category | flops | bytes accessed | tf_op | source)
XLA Modules:
  0.0 43.6 jit_solution(16592260048703638234)
XLA Ops:
  0.6 40.8 %grads.1 = (bf16[1,128,4096]{2,1,0:T(8,128)(2,1)}, bf16[1,128,512]{2,1,0:T(8,128)(2,1)}, bf16[1,128,512]{2,1,0:T(8,128)(2,1)}, bf16[48,512]{1,0:T(8,128)(2,1)}, bf16[48,512]{1,0:T(8,128)(2,1)}) custom-call(bf16[1,128,4096]{2,1,0:T(8,128)(2,1)} %q_hbm.1, bf16[1,128,4096]{2,1,0:T(8,128)(2,1)} %o_hbm.1, bf16[1,128,4096]{2,1,0:T(8,128)(2,1)} %g_hbm.1, ...), custom_call_target="tpu_custom_call" | custom-call | flops 4700000256 | bytes 5000000 | tf_op jit(solution)/shard_map/grads/pallas_call | solution.py:421
  41.5 2.2 %finish.1 = (bf16[1,128,4096]{2,1,0:T(8,128)(2,1)}, bf16[1,128,512]{2,1,0:T(8,128)(2,1)}, bf16[1,128,512]{2,1,0:T(8,128)(2,1)}, bf16[48,512]{1,0:T(8,128)(2,1)}, bf16[48,512]{1,0:T(8,128)(2,1)}) custom-call(bf16[1,128,4096]{2,1,0:T(8,128)(2,1)} %get-tuple-element.10.refs_0_, bf16[1,128,512]{2,1,0:T(8,128)(2,1)} %get-tuple-element.11.refs_1_, ...), custom_call_target="tpu_custom_call" | custom-call | tf_op jit(solution)/shard_map/finish/pallas_call | solution.py:468

commit v4 on v3

--- a/solution.py
+++ b/solution.py
@@ -144,9 +144,17 @@
     first = ((0, 1, 3), (1, -1, -3), (2, 2 * sign, 4), (3, 1, 1), (4, -1, -1))
 
     def scatter_a(h):
-        sib_out[h] = acc[half_of(1 - c)].astype(BF16)
+        i = h * PAIRS + PAIRS - 1
+
+        def summed(core):
+            rows = half_of(core)
+            value = dot(p_scr[PAIRS - 1, rows], two(g, i))
+            key = dot(ds_scr[i, rows], two(q, i)) * SCALE
+            return acc[rows] + jnp.concatenate([key, value], axis=1)
+
+        sib_out[h] = summed(1 - c).astype(BF16)
         sib_scatter(h).start()
-        cp[h] = acc[half_of(c)]
+        cp[h] = summed(c)
 
     def scatter_b(h):
         sib_scatter(h).wait_recv()
@@ -289,7 +297,7 @@
                 ahead = scores(h, p + 1, following)
             weave(exponents(h, p, state), ahead)
             weave(score_grads(h, p, state), pending)
-            pending = prompt_grads(h, p)
+            pending = prompt_grads(h, p) if p + 1 < PAIRS else []
             state = following
             if p < 2:
                 @pl.when(h == 0)
@@ -307,8 +315,6 @@
                 @pl.when(h >= 2)
                 def _():
                     scatter_c(h - 2)
-        for entry in pending:
-            entry()
         scatter_a(h)
         return 0
 

time: 44.1 us -> 43.7 us (level)
  no operation moved by 1% of the time
where the time goes in v4:
time: 43.7 us; the launch traced here: 43.4 us
  Pallas kernels  42.8 us (98%)
  between operations  0.64 us (1%)
    pallas_call x1, Pallas kernels, local(): pl.pallas_call(kernel, name='grads', out_shape=shapes, in_specs=[any_spec...  40.6 us
    pallas_call x1, Pallas kernels, local(): pl.pallas_call(finish, name='finish', out_shape=shapes, in_specs=[any_spe...  2.16 us

profile of v4, /device:TPU:2, one launch (start us, length us, event | category | flops | bytes accessed | tf_op | source)
XLA Modules:
  0.0 43.4 jit_solution(18279544833961980052)
XLA Ops:
  0.6 40.6 %grads.1 = (bf16[1,128,4096]{2,1,0:T(8,128)(2,1)}, bf16[1,128,512]{2,1,0:T(8,128)(2,1)}, bf16[1,128,512]{2,1,0:T(8,128)(2,1)}, bf16[48,512]{1,0:T(8,128)(2,1)}, bf16[48,512]{1,0:T(8,128)(2,1)}) custom-call(bf16[1,128,4096]{2,1,0:T(8,128)(2,1)} %q_hbm.1, bf16[1,128,4096]{2,1,0:T(8,128)(2,1)} %o_hbm.1, bf16[1,128,4096]{2,1,0:T(8,128)(2,1)} %g_hbm.1, ...), custom_call_target="tpu_custom_call" | custom-call | flops 4700000256 | bytes 5000000 | tf_op jit(solution)/shard_map/grads/pallas_call | solution.py:427
  41.3 2.2 %finish.1 = (bf16[1,128,4096]{2,1,0:T(8,128)(2,1)}, bf16[1,128,512]{2,1,0:T(8,128)(2,1)}, bf16[1,128,512]{2,1,0:T(8,128)(2,1)}, bf16[48,512]{1,0:T(8,128)(2,1)}, bf16[48,512]{1,0:T(8,128)(2,1)}) custom-call(bf16[1,128,4096]{2,1,0:T(8,128)(2,1)} %get-tuple-element.10.refs_0_, bf16[1,128,512]{2,1,0:T(8,128)(2,1)} %get-tuple-element.11.refs_1_, ...), custom_call_target="tpu_custom_call" | custom-call | tf_op jit(solution)/shard_map/finish/pallas_call | solution.py:474
